TPU v7x, 32 devices: a whole 2x2x4 slice. The times are simulated.
32 devices in a mesh: rows: 8 (over z, y), cols: 4 (over x, core).
Axes of the slice: x: 2, y: 2, z: 4, core: 2. Of those that a mesh axis runs over, the one named last changes fastest.
Arguments:
- tracks: float32 [1024, 2, 16384], P(('rows', 'cols')), may hold values from -200 to 200
- pixel_order: int32 [16384], P('rows'), may hold values from 0 to 16383, as said below
- pairing: int32 [2, 4], replicated, may hold values from 0 to 2
Outputs:
- rotated: float32 [16384, 2048], P('rows', 'cols')
Inputs may be any that keep to these rules, and one draw needn't show every extreme that they name: `pixel_order`: A permutation of 0 to 16383 that maps each aligned block of 2048 rows onto the same block of pixels.
All inputs are finite; a program needn't handle non-finite values.
Results may differ from a plain program's by a relative error of at most 0.0001.
Values sent between devices are 32-bit elements; how exact they have to be, the bound alone decides.
No kernel may reach another device: no remote copies, remote signals or barrier semaphores. Data moves between devices by JAX's collectives and lax.ppermute only.
A program may use at most 64 MiB of HBM per device.

v0:
```python
import functools

import jax
import jax.numpy as jnp
from jax import lax
from jax.experimental import pallas as pl
from jax.experimental.pallas import tpu as pltpu
from jax.sharding import PartitionSpec as P

STEPS = 2
NS_STEPS = 6
SLOTS = 4
MIB = 1024 * 1024

F32 = jnp.float32
BF16 = jnp.bfloat16
NN = (((1,), (0,)), ((), ()))
NT = (((1,), (1,)), ((), ()))
TN = (((0,), (0,)), ((), ()))


def pair_slots(chosen):
    partner = 2 - chosen
    low = jnp.where(partner == 0, 1, 0)
    high = jnp.where(partner == 2, 1, 2)
    return partner, low, high


def params(mib, flops=0, moved=0):
    return dict(
        compiler_params=pltpu.CompilerParams(vmem_limit_bytes=mib * MIB),
        cost_estimate=pl.CostEstimate(flops=int(flops), bytes_accessed=int(moved), transcendentals=0),
    )


def halves(value):
    high = value.astype(BF16)
    return high, (value - high.astype(F32)).astype(BF16)


def mul(a, b, dims):
    return lax.dot_general(a, b, dims, preferred_element_type=F32)


def dot_split(a, b, dims):
    a_high, a_low = halves(a)
    b_high, b_low = halves(b)
    return mul(a_high, b_high, dims) + (mul(a_high, b_low, dims) + mul(a_low, b_high, dims))


def dot_full(a, b, dims=NN):
    return lax.dot_general(a, b, dims, precision=lax.Precision.HIGHEST, preferred_element_type=F32)


def identity(size):
    return lax.broadcasted_iota(jnp.int32, (size, size), 0) == lax.broadcasted_iota(jnp.int32, (size, size), 1)


LANES = 128
WAYS = 4


def block_rows(refs, slot):
    width = refs[0].shape[0] // SLOTS
    return jnp.concatenate([ref[pl.ds(slot, width, SLOTS), :] for ref in refs], axis=1)


def lane_specs(columns):
    return [pl.BlockSpec((columns, LANES), lambda k, way=way: (0, WAYS * k + way)) for way in range(WAYS)]


def at(ref, row, column, width):
    rows = pl.ds(pl.multiple_of(row * width, width), width)
    columns = pl.ds(pl.multiple_of(column * width, width), width)
    return ref[rows, columns]


def spread_kernel(tracks_ref, pieces_ref):
    frames = tracks_ref.shape[0]
    for component in range(2):
        plane = tracks_ref[:, component, :]
        for group in range(frames // 8):
            for half in range(2):
                pieces_ref[0, 2 * component + half, 4 * group:4 * group + 4, :] = plane[
                    8 * group + 4 * half:8 * group + 4 * half + 4, :]


def spread(tracks, row_devices):
    frames, _, pixels = tracks.shape
    rows = pixels // row_devices
    return pl.pallas_call(
        spread_kernel,
        grid=(row_devices,),
        in_specs=[pl.BlockSpec((frames, 2, rows), lambda r: (0, 0, r))],
        out_specs=pl.BlockSpec((1, 4, frames // 2, rows), lambda r: (r, 0, 0, 0)),
        out_shape=jax.ShapeDtypeStruct((row_devices, 4, frames // 2, rows), F32),
        name="spread",
        **params(16, 0, 8 * tracks.size),
    )(tracks)


def gram_kernel(chosen_ref, *refs):
    held_refs, (sums_ref, gram_ref, last_ref, cross_ref) = refs[:WAYS], refs[WAYS:]
    step = pl.program_id(0)
    width = sums_ref.shape[1]
    high, low = halves(jnp.concatenate([block_rows(held_refs, b) for b in range(SLOTS)], axis=0))
    partner, first, second = pair_slots(chosen_ref[0])
    last_ref[:width, :] = block_rows(held_refs, partner)
    last_ref[width:, :] = block_rows(held_refs, SLOTS - 1)

    @pl.when(step == 0)
    def _():
        gram_ref[...] = jnp.zeros_like(gram_ref)
        cross_ref[...] = jnp.zeros_like(cross_ref)

    gram_ref[...] += mul(high, high, NT)
    cross_ref[...] += mul(high, low, NT)

    @pl.when(step == pl.num_programs(0) - 1)
    def _():
        cross = cross_ref[...]
        gram_ref[...] += cross + cross.T
        sums_ref[:width, :] = at(gram_ref, partner, SLOTS - 1, width)
        sums_ref[width:2 * width, :] = at(gram_ref, first, second, width)
        on_diagonal = identity(width)
        slots = (partner, SLOTS - 1, first, second)
        sums = [jnp.sum(jnp.where(on_diagonal, at(gram_ref, s, s, width), 0.0), axis=0, keepdims=True) for s in slots]
        sums_ref[2 * width:, :] = jnp.concatenate(sums + [jnp.zeros((4, width), F32)], axis=0)


def local_gram(chosen, held):
    columns, rows = held.shape
    width = columns // SLOTS
    chunk = WAYS * LANES
    return pl.pallas_call(
        gram_kernel,
        grid=(rows // chunk,),
        in_specs=[pl.BlockSpec(memory_space=pltpu.SMEM)] + lane_specs(columns),
        out_specs=[
            pl.BlockSpec((2 * width + 8, width), lambda k: (0, 0)),
            pl.BlockSpec((columns, columns), lambda k: (0, 0)),
            pl.BlockSpec((2 * width, chunk), lambda k: (0, k)),
        ],
        out_shape=[
            jax.ShapeDtypeStruct((2 * width + 8, width), F32),
            jax.ShapeDtypeStruct((columns, columns), F32),
            jax.ShapeDtypeStruct((2 * width, rows), F32),
        ],
        scratch_shapes=[pltpu.VMEM((columns, columns), F32)],
        name="gram",
        **params(32, 4 * columns * columns * rows, 6 * held.size),
    )(chosen, *[held] * WAYS)


def cross_kernel(chosen_ref, *refs):
    held_refs, (came_ref, cross_ref, own_ref) = refs[:WAYS], refs[WAYS:]
    step = pl.program_id(0)
    partner, first, second = pair_slots(chosen_ref[0])
    meets = 2 - chosen_ref[1]
    in_last = meets == partner
    one = jnp.where(in_last, partner, first)
    two = jnp.where(in_last, SLOTS - 1, second)
    here = jnp.concatenate([block_rows(held_refs, s) for s in (one, two)], axis=0)
    here_high, here_low = halves(here)
    came_high, came_low = halves(came_ref[...])
    cross = mul(here_high, came_high, NT) + (mul(here_high, came_low, NT) + mul(here_low, came_high, NT))
    twice = mul(came_high, came_low, NT)
    own = mul(came_high, came_high, NT) + (twice + twice.T)

    @pl.when(step == 0)
    def _():
        cross_ref[...] = cross
        own_ref[...] = own

    @pl.when(step > 0)
    def _():
        cross_ref[...] += cross
        own_ref[...] += own


def cross_gram(chosen, held, came):
    columns, rows = held.shape
    pair = came.shape[0]
    chunk = WAYS * LANES
    square = jax.ShapeDtypeStruct((pair, pair), F32)
    return pl.pallas_call(
        cross_kernel,
        grid=(rows // chunk,),
        in_specs=[pl.BlockSpec(memory_space=pltpu.SMEM)] + lane_specs(columns) + [
            pl.BlockSpec((pair, chunk), lambda k: (0, k))],
        out_specs=[pl.BlockSpec((pair, pair), lambda k: (0, 0))] * 2,
        out_shape=[square, square],
        name="cross_gram",
        **params(32, 10 * pair * pair * rows, 6 * held.size),
    )(chosen, *[held] * WAYS, came)


def rotations(grams):
    width = grams[0][0].shape[0]
    eye = identity(width).astype(F32)
    couplings, scales, squares, products = [], [], [], []
    for block, row_sums, column_sums in grams:
        spread_sums = jnp.broadcast_to(row_sums, (width, width)).T
        coupling = block / (spread_sums + column_sums)
        total = 1.0 + jnp.sum(coupling * coupling)
        couplings.append(coupling)
        for dims in (NT, TN):
            scales.append(1.0 / jnp.sqrt(total))
            squares.append((eye + dot_full(coupling, coupling, dims)) / total)
    for count in range(NS_STEPS):
        factors = [1.5 * eye - 0.5 * square for square in squares]
        if count == 0:
            products = [scale * factor for scale, factor in zip(scales, factors)]
        else:
            products = [dot_full(product, factor) for product, factor in zip(products, factors)]
        if count + 1 < NS_STEPS:
            squares = [dot_full(square, factor) for square, factor in zip(squares, factors)]
            squares = [dot_full(square, factor) for square, factor in zip(squares, factors)]
    results = []
    for index, coupling in enumerate(couplings):
        across = dot_full(products[2 * index], coupling)
        results.append((products[2 * index], across, -across.T, products[2 * index + 1]))
    return results


def rotation_kernel(sums_ref, came_ref, rotation_ref):
    width = sums_ref.shape[1]
    sums = sums_ref[2 * width:, :]
    came = came_ref[width:, :]
    grams = [
        (sums_ref[:width, :], sums[0:1], sums[1:2]),
        (sums_ref[width:2 * width, :], sums[2:3], sums[3:4]),
        (came_ref[:width, :], came[0:1], came[1:2]),
    ]
    for index, (top, right, bottom, end) in enumerate(rotations(grams)):
        rotation_ref[index, :width, :width] = top
        rotation_ref[index, :width, width:] = right
        rotation_ref[index, width:, :width] = bottom
        rotation_ref[index, width:, width:] = end


def three_rotations(sums, came):
    width = sums.shape[1]
    return pl.pallas_call(
        rotation_kernel,
        out_shape=jax.ShapeDtypeStruct((3, 2 * width, 2 * width), F32),
        name="rotations",
        **params(16, 200 * 6 * width**3, 16 * width * width),
    )(sums, came)


def second_kernel(chosen_ref, gram_ref, cross_ref, own_ref, rotation_ref, sums_ref):
    width = sums_ref.shape[1]
    partner, first, second = pair_slots(chosen_ref[0])
    meets, low, high = pair_slots(chosen_ref[1])

    def place(slot):
        in_last = slot == partner
        members = (jnp.where(in_last, partner, first), jnp.where(in_last, SLOTS - 1, second))
        columns = jnp.where(jnp.logical_or(in_last, slot == first), 0, 1)
        turn = rotation_ref[jnp.where(in_last, 0, 1), :, pl.ds(pl.multiple_of(columns * width, width), width)]
        return members, turn

    def between(rows, columns):
        return jnp.concatenate(
            [jnp.concatenate([at(gram_ref, r, c, width) for c in columns], axis=1) for r in rows], axis=0)

    (meets_in, meets_turn), (low_in, low_turn), (high_in, high_turn) = place(meets), place(low), place(high)
    came_turn = rotation_ref[2, :, width:]
    sums_ref[:width, :] = dot_split(meets_turn, dot_split(cross_ref[...], came_turn, NN), TN)
    sums_ref[width:2 * width, :] = dot_split(low_turn, dot_split(between(low_in, high_in), high_turn, NN), TN)

    def squares(gram, turn):
        return jnp.sum(turn * dot_split(gram, turn, NN), axis=0, keepdims=True)

    rows = [
        squares(between(meets_in, meets_in), meets_turn),
        squares(own_ref[...], came_turn),
        squares(between(low_in, low_in), low_turn),
        squares(between(high_in, high_in), high_turn),
        jnp.zeros((4, width), F32),
    ]
    sums_ref[2 * width:, :] = jnp.concatenate(rows, axis=0)


def second_sums(chosen, gram, cross, own, turns):
    width = gram.shape[0] // SLOTS
    vmem = pl.BlockSpec(memory_space=pltpu.VMEM)
    return pl.pallas_call(
        second_kernel,
        in_specs=[pl.BlockSpec(memory_space=pltpu.SMEM)] + [vmem] * 4,
        out_specs=vmem,
        out_shape=jax.ShapeDtypeStruct((2 * width + 8, width), F32),
        name="second_sums",
        **params(16, 6 * 32 * width**3, 16 * gram.size),
    )(chosen, gram, cross, own, turns)


def picks(order_ref, rows):
    order = order_ref[...]
    return jnp.where(lax.broadcasted_iota(jnp.int32, (rows, order.shape[1]), 0) == order, 1.0, 0.0).astype(BF16)


def order_kernel(order_ref, held_ref, matrix_ref, split_ref, turned_ref):
    columns, rows = held_ref.shape
    width = columns // SLOTS

    @pl.when(pl.program_id(0) == 0)
    def _():
        high, low = halves(held_ref[...])
        split_ref[:columns, :] = high
        split_ref[columns:, :] = low

    both = mul(split_ref[...], picks(order_ref, rows), NN)
    both = both[:columns] + both[columns:]
    for part in range(matrix_ref.shape[1] // LANES):
        lanes = slice(part * LANES, (part + 1) * LANES)
        turned_ref[part] = both[:, lanes]
        for block in range(SLOTS):
            matrix_ref[block, lanes, :] = turned_ref[part, pl.ds(block, width, SLOTS), :].T


def ordered(order, held):
    columns, rows = held.shape
    width = columns // SLOTS
    chunk = 2 * width
    return pl.pallas_call(
        order_kernel,
        grid=(rows // chunk,),
        in_specs=[
            pl.BlockSpec((1, chunk), lambda k: (0, k)),
            pl.BlockSpec((columns, rows), lambda k: (0, 0)),
        ],
        out_specs=pl.BlockSpec((SLOTS, chunk, width), lambda k: (0, k, 0)),
        out_shape=jax.ShapeDtypeStruct((SLOTS, rows, width), F32),
        scratch_shapes=[pltpu.VMEM((2 * columns, rows), BF16), pltpu.VMEM((chunk // LANES, columns, LANES), F32)],
        name="row_order",
        **params(40, 4 * columns * rows * rows, 8 * held.size),
    )(order, held)


def turn_kernel(chosen_ref, matrix_ref, rotation_ref, turned_ref, meets_ref):
    width = matrix_ref.shape[2]
    partner, first, second = pair_slots(chosen_ref[0])
    for index, (one, two) in enumerate(((partner, SLOTS - 1), (first, second))):
        pair = jnp.concatenate([matrix_ref[one], matrix_ref[two]], axis=1)
        turned = dot_split(pair, rotation_ref[index], NN)
        turned_ref[one] = turned[:, :width]
        turned_ref[two] = turned[:, width:]
    meets_ref[...] = turned_ref[2 - chosen_ref[1]]


def turn(chosen, matrix, turns):
    _, rows, width = matrix.shape
    chunk = rows // 4
    return pl.pallas_call(
        turn_kernel,
        grid=(rows // chunk,),
        in_specs=[
            pl.BlockSpec(memory_space=pltpu.SMEM),
            pl.BlockSpec((SLOTS, chunk, width), lambda k: (0, k, 0)),
            pl.BlockSpec(turns.shape, lambda k: (0, 0, 0)),
        ],
        out_specs=[
            pl.BlockSpec((SLOTS, chunk, width), lambda k: (0, k, 0)),
            pl.BlockSpec((chunk, width), lambda k: (k, 0)),
        ],
        out_shape=[jax.ShapeDtypeStruct(matrix.shape, F32), jax.ShapeDtypeStruct((rows, width), F32)],
        name="first_turn",
        **params(32, 24 * rows * width * width, 9 * matrix.size),
    )(chosen, matrix, turns)


def moved_kernel(order_ref, came_ref, rotation_ref, block_ref, split_ref):
    width = block_ref.shape[1]
    rows = came_ref.shape[1]

    @pl.when(pl.program_id(0) == 0)
    def _():
        high, low = halves(dot_split(rotation_ref[2, :, width:], came_ref[...], TN))
        split_ref[:width, :] = high
        split_ref[width:, :] = low

    both = mul(split_ref[...], picks(order_ref, rows), NN)
    block_ref[...] = (both[:width] + both[width:]).T


def moved_block(order, came, turns):
    pair, rows = came.shape
    width = pair // 2
    chunk = pair
    return pl.pallas_call(
        moved_kernel,
        grid=(rows // chunk,),
        in_specs=[
            pl.BlockSpec((1, chunk), lambda k: (0, k)),
            pl.BlockSpec((pair, rows), lambda k: (0, 0)),
            pl.BlockSpec(turns.shape, lambda k: (0, 0, 0)),
        ],
        out_specs=pl.BlockSpec((chunk, width), lambda k: (k, 0)),
        out_shape=jax.ShapeDtypeStruct((rows, width), F32),
        scratch_shapes=[pltpu.VMEM((pair, rows), BF16)],
        name="moved_block",
        **params(32, 4 * width * rows * rows, 8 * came.size),
    )(order, came, turns)


def finish_kernel(chosen_ref, turned_ref, moved_ref, behind_ref, rotation_ref, out_ref):
    width = moved_ref.shape[1]
    meets, low, high = pair_slots(chosen_ref[1])

    def put(slot, value):
        out_ref[:, pl.ds(pl.multiple_of(slot * width, width), width)] = value

    pair = dot_split(jnp.concatenate([turned_ref[low], turned_ref[high]], axis=1), rotation_ref[1], NN)
    put(low, pair[:, :width])
    put(high, pair[:, width:])
    put(meets, dot_split(
        jnp.concatenate([turned_ref[meets], moved_ref[...]], axis=1), rotation_ref[0, :, :width], NN))
    put(SLOTS - 1, dot_split(
        jnp.concatenate([behind_ref[...], turned_ref[SLOTS - 1]], axis=1), rotation_ref[2, :, width:], NN))


def finish(chosen, turned, moved, behind, turns):
    _, rows, width = turned.shape
    chunk = rows // 4
    block = pl.BlockSpec((chunk, width), lambda k: (k, 0))
    return pl.pallas_call(
        finish_kernel,
        grid=(rows // chunk,),
        in_specs=[
            pl.BlockSpec(memory_space=pltpu.SMEM),
            pl.BlockSpec((SLOTS, chunk, width), lambda k: (0, k, 0)),
            block,
            block,
            pl.BlockSpec(turns.shape, lambda k: (0, 0, 0)),
        ],
        out_specs=pl.BlockSpec((chunk, SLOTS * width), lambda k: (k, 0)),
        out_shape=jax.ShapeDtypeStruct((rows, SLOTS * width), F32),
        name="second_turn",
        **params(32, 24 * rows * width * width, 10 * turned.size),
    )(chosen, turned, moved, behind, turns)


def from_behind(value, axis, steps):
    count = lax.axis_size(axis)
    pairs = [(source, (source + steps) % count) for source in range(count)]
    return lax.ppermute(value, axis, pairs)


def summed(value, axis):
    count = lax.axis_size(axis)
    if count & (count - 1):
        return lax.psum(value, axis)
    distance = 1
    while distance < count:
        pairs = [(source, source ^ distance) for source in range(count)]
        value = value + lax.ppermute(value, axis, pairs)
        distance *= 2
    return value


def last_pair(sums):
    width = sums.shape[1]
    return jnp.concatenate([sums[:width], sums[2 * width:]], axis=0)


def body(tracks, pixel_order, pairing):
    frames_dev, _, pixel_total = tracks.shape
    row_devices = lax.axis_size("rows")
    row_count = pixel_total // row_devices
    pieces = spread(tracks, row_devices).reshape(row_devices * 4, frames_dev // 2, row_count)
    arrived = lax.all_to_all(pieces, ("rows", "cols"), split_axis=0, concat_axis=0, tiled=True)
    held = arrived.reshape(-1, row_count)
    order = (pixel_order - lax.axis_index("rows") * row_count).reshape(1, row_count)
    chosen = lax.dynamic_index_in_dim(pairing, lax.axis_index("cols"), axis=1, keepdims=False)

    sums, gram, last = local_gram(chosen, held)
    came = from_behind(last, "cols", 1)
    sums = summed(sums, "rows")
    matrix = ordered(order, held)
    came_sums = from_behind(last_pair(sums), "cols", 1)
    turns = three_rotations(sums, came_sums)
    cross, own = cross_gram(chosen, held, came)

    sums = summed(second_sums(chosen, gram, cross, own, turns), "rows")
    turned, meets = turn(chosen, matrix, turns)
    behind = from_behind(meets, "cols", -1)
    moved = moved_block(order, came, turns)
    behind_sums = from_behind(last_pair(sums), "cols", -1)
    turns = three_rotations(sums, behind_sums)
    return finish(chosen, turned, moved, behind, turns)


def solution(mesh):
    placed = (P(("rows", "cols"), None, None), P("rows"), P())
    return jax.shard_map(
        body, mesh=mesh, in_specs=placed, out_specs=P("rows", "cols"), check_vma=False
    )
```

profile of v0, /device:TPU:1, one launch (start us, length us, event | category | flops | bytes accessed | tf_op | source)
XLA Modules:
  0.0 201.2 jit_solution(15485462465455301086)
XLA Ops:
  0.0 0.0 copy-start
  0.0 0.0 copy-start.2
  0.0 2.2 %copy-done.2 = f32[32,2,16384]{2,1,0:T(2,128)S(1)} copy-done((f32[32,2,16384]{2,1,0:T(2,128)S(1)}, f32[32,2,16384]{2,1,0:T(2,128)}, u32[]{:S(2)}) %copy-start.2) | copy-done | bytes 4194328
  2.2 1.2 spread.1
  3.4 0.0 copy-start.1
  3.4 2.0 copy-done.1
  5.4 7.2 %all-to-all-start = ((f32[32,16,2048]{2,1,0:T(8,128)}), f32[32,16,2048]{2,1,0:T(8,128)}, u32[]{:S(2)}, u32[]{:S(2)}) async-start(f32[32,16,2048]{2,1,0:T(8,128)} %bitcast.3), calls=%async_computation | async-start | bytes 8388608 | tf_op jit(solution)/shard_map/all_to_all | solution.py:473
  12.6 0.0 copy-done
  12.6 0.2 dynamic-slice_reduce_fusion.chosen_ref
  12.8 93.1 %all-to-all-done = f32[32,16,2048]{2,1,0:T(8,128)} async-done(((f32[32,16,2048]{2,1,0:T(8,128)}), f32[32,16,2048]{2,1,0:T(8,128)}, u32[]{:S(2)}, u32[]{:S(2)}) %all-to-all-start) | async-done | bytes 4194336 | tf_op jit(solution)/shard_map/all_to_all | solution.py:473
  105.9 0.0 copy-start.3
  105.9 7.2 %gram.1 = (f32[264,128]{1,0:T(8,128)S(1)}, f32[512,512]{1,0:T(8,128)S(1)}, f32[256,2048]{1,0:T(8,128)}) custom-call(s32[2]{0:T(128)S(1)} %dynamic-slice_reduce_fusion.chosen_ref, f32[512,2048]{1,0:T(8,128)} %bitcast.2.held_ref.refs_0_.refs_1_.refs_2_.refs_3_, f32[512,2048]{1,0:T(8,128)} %bitcast.2.held_ref.refs_0_.refs_1_.refs_2_.refs_3_, ...), custom_call_target="tpu_custom_call" | custom-call | flops 2147483648 | bytes 6291456 | tf_op jit(solution)/shard_map/gram/pallas_call | solution.py:135
  113.1 1.7 collective-permute-start.4
  114.9 1.4 collective-permute-start
  116.3 3.8 %collective-permute-done = f32[264,128]{1,0:T(8,128)S(1)} collective-permute-done((f32[264,128]{1,0:T(8,128)S(1)}, f32[264,128]{1,0:T(8,128)S(1)}, u32[]{:S(2)}, u32[]{:S(2)}) %collective-permute-start) | collective-permute-done | bytes 135200 | tf_op jit(solution)/shard_map/ppermute | solution.py:458
  120.1 0.1 collective-permute-start.1
  120.2 5.1 %collective-permute-done.1 = f32[264,128]{1,0:T(8,128)S(1)} collective-permute-done((f32[264,128]{1,0:T(8,128)S(1)}, f32[264,128]{1,0:T(8,128)S(1)}, u32[]{:S(2)}, u32[]{:S(2)}) %collective-permute-start.1) | collective-permute-done | bytes 135200 | tf_op jit(solution)/shard_map/ppermute | solution.py:458
  125.3 0.7 collective-permute-start.2
  126.0 0.0 copy-done.3
  126.0 8.6 %collective-permute-done.2 = f32[264,128]{1,0:T(8,128)S(1)} collective-permute-done((f32[264,128]{1,0:T(8,128)S(1)}, f32[264,128]{1,0:T(8,128)S(1)}, u32[]{:S(2)}, u32[]{:S(2)}) %collective-permute-start.2) | collective-permute-done | bytes 135200 | tf_op jit(solution)/shard_map/ppermute | solution.py:458
  134.7 0.8 collective-permute-start.3
  135.4 14.8 %row_order.1.matrix_ref = f32[4,2048,128]{2,1,0:T(8,128)S(1)} custom-call(s32[1,2048]{1,0:T(1,128)S(1)} %bitcast.4, f32[512,2048]{1,0:T(8,128)} %bitcast.2.held_ref.refs_0_.refs_1_.refs_2_.refs_3_), custom_call_target="tpu_custom_call" | custom-call | flops 8589934592 | bytes 8388608 | tf_op jit(solution)/shard_map/row_order/pallas_call | solution.py:327
  150.2 0.0 collective-permute-done.3.came_ref
  150.2 5.8 %rotations.2.rotation_ref = f32[3,256,256]{2,1,0:T(8,128)S(1)} custom-call(f32[264,128]{1,0:T(8,128)S(1)} %add.25.sums_ref, f32[136,128]{1,0:T(8,128)S(1)} %collective-permute-done.3.came_ref), custom_call_target="tpu_custom_call" | custom-call | flops 2516582400 | bytes 262144 | tf_op jit(solution)/shard_map/rotations/pallas_call | solution.py:244
  156.1 3.8 %first_turn.1 = (f32[4,2048,128]{2,1,0:T(8,128)S(1)}, f32[2048,128]{1,0:T(8,128)S(1)}) custom-call(s32[2]{0:T(128)S(1)} %dynamic-slice_reduce_fusion.chosen_ref, f32[4,2048,128]{2,1,0:T(8,128)S(1)} %row_order.1.matrix_ref, f32[3,256,256]{2,1,0:T(8,128)S(1)} %rotations.2.rotation_ref), custom_call_target="tpu_custom_call" | custom-call | flops 805306368 | bytes 9437184 | tf_op jit(solution)/shard_map/first_turn/pallas_call | solution.py:356
  159.9 0.2 collective-permute-start.5
  160.2 0.0 collective-permute-done.4.came_ref.refs_4_
  160.2 4.5 %cross_gram.1 = (f32[256,256]{1,0:T(8,128)S(1)}, f32[256,256]{1,0:T(8,128)S(1)}) custom-call(s32[2]{0:T(128)S(1)} %dynamic-slice_reduce_fusion.chosen_ref, f32[512,2048]{1,0:T(8,128)} %bitcast.2.held_ref.refs_0_.refs_1_.refs_2_.refs_3_, f32[512,2048]{1,0:T(8,128)} %bitcast.2.held_ref.refs_0_.refs_1_.refs_2_.refs_3_, ...), custom_call_target="tpu_custom_call" | custom-call | flops 1342177280 | bytes 6291456 | tf_op jit(solution)/shard_map/cross_gram/pallas_call | solution.py:186
  164.7 1.8 second_sums.1
  166.5 0.8 collective-permute-start.6
  167.3 3.2 %collective-permute-done.6 = f32[264,128]{1,0:T(8,128)S(1)} collective-permute-done((f32[264,128]{1,0:T(8,128)S(1)}, f32[264,128]{1,0:T(8,128)S(1)}, u32[]{:S(2)}, u32[]{:S(2)}) %collective-permute-start.6) | collective-permute-done | bytes 135200 | tf_op jit(solution)/shard_map/ppermute | solution.py:458
  170.5 0.1 collective-permute-start.7
  170.5 3.8 %collective-permute-done.7 = f32[264,128]{1,0:T(8,128)S(1)} collective-permute-done((f32[264,128]{1,0:T(8,128)S(1)}, f32[264,128]{1,0:T(8,128)S(1)}, u32[]{:S(2)}, u32[]{:S(2)}) %collective-permute-start.7) | collective-permute-done | bytes 135200 | tf_op jit(solution)/shard_map/ppermute | solution.py:458
  174.4 0.8 collective-permute-start.8
  175.2 5.2 %collective-permute-done.8 = f32[264,128]{1,0:T(8,128)S(1)} collective-permute-done((f32[264,128]{1,0:T(8,128)S(1)}, f32[264,128]{1,0:T(8,128)S(1)}, u32[]{:S(2)}, u32[]{:S(2)}) %collective-permute-start.8) | collective-permute-done | bytes 135200 | tf_op jit(solution)/shard_map/ppermute | solution.py:458
  180.5 4.7 %collective-permute-start.9 = (f32[136,128]{1,0:T(8,128)S(1)}, f32[136,128]{1,0:T(8,128)S(1)}, u32[]{:S(2)}, u32[]{:S(2)}) collective-permute-start(f32[136,128]{1,0:T(8,128)S(1)} %pad_maximum_fusion.1), channel_id=1, source_target_pairs={{0,3},{1,0},{2,1},{3,2},{4,7},{5,4},{6,5},{7,6},{8,11},{9,8},{10,9... | collective-permute-start | bytes 208904 | tf_op jit(solution)/shard_map/ppermute | solution.py:448
  185.1 5.0 %moved_block.1.moved_ref = f32[2048,128]{1,0:T(8,128)S(1)} custom-call(s32[1,2048]{1,0:T(1,128)S(1)} %bitcast.5, f32[256,2048]{1,0:T(8,128)S(1)} %collective-permute-done.4.came_ref.refs_4_, f32[3,256,256]{2,1,0:T(8,128)S(1)} %rotations.2.rotation_ref), custom_call_target="tpu_custom_call" | custom-call | flops 2147483648 | bytes 4194304 | tf_op jit(solution)/shard_map/moved_block/pallas_call | solution.py:392
  190.1 0.0 collective-permute-done.9.came_ref
  190.1 5.8 %rotations.3.rotation_ref = f32[3,256,256]{2,1,0:T(8,128)S(1)} custom-call(f32[264,128]{1,0:T(8,128)S(1)} %add.28.sums_ref, f32[136,128]{1,0:T(8,128)S(1)} %collective-permute-done.9.came_ref), custom_call_target="tpu_custom_call" | custom-call | flops 2516582400 | bytes 262144 | tf_op jit(solution)/shard_map/rotations/pallas_call | solution.py:244
  196.0 0.0 collective-permute-done.5.behind_ref
  196.0 5.2 %second_turn.1 = f32[2048,512]{1,0:T(8,128)} custom-call(s32[2]{0:T(128)S(1)} %dynamic-slice_reduce_fusion.chosen_ref, f32[4,2048,128]{2,1,0:T(8,128)S(1)} %get-tuple-element.13.turned_ref, f32[2048,128]{1,0:T(8,128)S(1)} %moved_block.1.moved_ref, f32[2048,128]{1,0:T(8,128)S(1)} %collective-permute-done.5.behind_ref, f32[3,256,256]{2,1,0:T(8,128)S(1)} %rotations.3.rotation_ref), custom_call_target="tpu_custom_call" | custom-call | flops 805306368 | bytes 10485760 | tf_op jit(solution)/shard_map/second_turn/pallas_call | solution.py:428
  (13 shorter events, 0.2 us)
Async XLA Ops:
  0.0 12.6 %copy-start = (s32[2,4]{1,0:T(2,128)S(1)}, s32[2,4]{1,0:T(2,128)}, u32[]{:S(2)}) copy-start(s32[2,4]{1,0:T(2,128)} %param.5) | copy-start | bytes 100
  0.0 2.2 %copy-start.2 = (f32[32,2,16384]{2,1,0:T(2,128)S(1)}, f32[32,2,16384]{2,1,0:T(2,128)}, u32[]{:S(2)}) copy-start(f32[32,2,16384]{2,1,0:T(2,128)} %tracks_ref.1) | copy-start | bytes 12582916
  3.4 2.0 %copy-start.1 = (f32[8,4,16,2048]{3,2,1,0:T(8,128)}, f32[8,4,16,2048]{3,2,1,0:T(8,128)S(1)}, u32[]{:S(2)}) copy-start(f32[8,4,16,2048]{3,2,1,0:T(8,128)S(1)} %spread.1) | copy-start | bytes 12582916
  5.4 100.5 %all-to-all-start = ((f32[32,16,2048]{2,1,0:T(8,128)}), f32[32,16,2048]{2,1,0:T(8,128)}, u32[]{:S(2)}, u32[]{:S(2)}) async-start(f32[32,16,2048]{2,1,0:T(8,128)} %bitcast.3), calls=%async_computation | async-start | bytes 8388608 | tf_op jit(solution)/shard_map/all_to_all | solution.py:473
  105.9 20.1 %copy-start.3 = (s32[2048]{0:T(1024)S(1)}, s32[2048]{0:T(1024)}, u32[]{:S(2)}) copy-start(s32[2048]{0:T(1024)} %param.4) | copy-start | bytes 24580
  113.1 47.0 %collective-permute-start.4 = (f32[256,2048]{1,0:T(8,128)}, f32[256,2048]{1,0:T(8,128)S(1)}, u32[]{:S(2)}, u32[]{:S(2)}) collective-permute-start(f32[256,2048]{1,0:T(8,128)} %get-tuple-element.14), channel_id=1, source_target_pairs={{0,1},{1,2},{2,3},{3,0},{4,5},{5,6},{6,7},{7,4},{8,9},{9,10},{10,1... | collective-permute-start | bytes 6291464 | tf_op jit(solution)/shard_map/ppermute | solution.py:448
  114.9 5.2 %collective-permute-start = (f32[264,128]{1,0:T(8,128)S(1)}, f32[264,128]{1,0:T(8,128)S(1)}, u32[]{:S(2)}, u32[]{:S(2)}) collective-permute-start(f32[264,128]{1,0:T(8,128)S(1)} %get-tuple-element.12), channel_id=1, source_target_pairs={{0,4},{4,0},{8,12},{12,8},{16,20},{20,16},{24,28},{28,24},{1,5},{5... | collective-permute-start | bytes 405512 | tf_op jit(solution)/shard_map/ppermute | solution.py:458
  120.1 5.2 %collective-permute-start.1 = (f32[264,128]{1,0:T(8,128)S(1)}, f32[264,128]{1,0:T(8,128)S(1)}, u32[]{:S(2)}, u32[]{:S(2)}) collective-permute-start(f32[264,128]{1,0:T(8,128)S(1)} %add.23), channel_id=1, source_target_pairs={{0,8},{4,12},{8,0},{12,4},{16,24},{20,28},{24,16},{28,20},{1,9},{5... | collective-permute-start | bytes 405512 | tf_op jit(solution)/shard_map/ppermute | solution.py:458
  125.3 9.3 %collective-permute-start.2 = (f32[264,128]{1,0:T(8,128)S(1)}, f32[264,128]{1,0:T(8,128)S(1)}, u32[]{:S(2)}, u32[]{:S(2)}) collective-permute-start(f32[264,128]{1,0:T(8,128)S(1)} %add.24), channel_id=1, source_target_pairs={{0,16},{4,20},{8,24},{12,28},{16,0},{20,4},{24,8},{28,12},{1,17},{... | collective-permute-start | bytes 405512 | tf_op jit(solution)/shard_map/ppermute | solution.py:458
  134.7 15.6 %collective-permute-start.3 = (f32[136,128]{1,0:T(8,128)S(1)}, f32[136,128]{1,0:T(8,128)S(1)}, u32[]{:S(2)}, u32[]{:S(2)}) collective-permute-start(f32[136,128]{1,0:T(8,128)S(1)} %pad_maximum_fusion), channel_id=1, source_target_pairs={{0,1},{1,2},{2,3},{3,0},{4,5},{5,6},{6,7},{7,4},{8,9},{9,10},{10,1... | collective-permute-start | bytes 208904 | tf_op jit(solution)/shard_map/ppermute | solution.py:448
  159.9 36.0 %collective-permute-start.5 = (f32[2048,128]{1,0:T(8,128)S(1)}, f32[2048,128]{1,0:T(8,128)S(1)}, u32[]{:S(2)}, u32[]{:S(2)}) collective-permute-start(f32[2048,128]{1,0:T(8,128)S(1)} %get-tuple-element.15), channel_id=1, source_target_pairs={{0,3},{1,0},{2,1},{3,2},{4,7},{5,4},{6,5},{7,6},{8,11},{9,8},{10,9... | collective-permute-start | bytes 3145736 | tf_op jit(solution)/shard_map/ppermute | solution.py:448
  166.5 3.9 %collective-permute-start.6 = (f32[264,128]{1,0:T(8,128)S(1)}, f32[264,128]{1,0:T(8,128)S(1)}, u32[]{:S(2)}, u32[]{:S(2)}) collective-permute-start(f32[264,128]{1,0:T(8,128)S(1)} %second_sums.1), channel_id=1, source_target_pairs={{0,4},{4,0},{8,12},{12,8},{16,20},{20,16},{24,28},{28,24},{1,5},{5... | collective-permute-start | bytes 405512 | tf_op jit(solution)/shard_map/ppermute | solution.py:458
  170.5 3.9 %collective-permute-start.7 = (f32[264,128]{1,0:T(8,128)S(1)}, f32[264,128]{1,0:T(8,128)S(1)}, u32[]{:S(2)}, u32[]{:S(2)}) collective-permute-start(f32[264,128]{1,0:T(8,128)S(1)} %add.26), channel_id=1, source_target_pairs={{0,8},{4,12},{8,0},{12,4},{16,24},{20,28},{24,16},{28,20},{1,9},{5... | collective-permute-start | bytes 405512 | tf_op jit(solution)/shard_map/ppermute | solution.py:458
  174.4 6.0 %collective-permute-start.8 = (f32[264,128]{1,0:T(8,128)S(1)}, f32[264,128]{1,0:T(8,128)S(1)}, u32[]{:S(2)}, u32[]{:S(2)}) collective-permute-start(f32[264,128]{1,0:T(8,128)S(1)} %add.27), channel_id=1, source_target_pairs={{0,16},{4,20},{8,24},{12,28},{16,0},{20,4},{24,8},{28,12},{1,17},{... | collective-permute-start | bytes 405512 | tf_op jit(solution)/shard_map/ppermute | solution.py:458
  180.5 9.7 %collective-permute-start.9 = (f32[136,128]{1,0:T(8,128)S(1)}, f32[136,128]{1,0:T(8,128)S(1)}, u32[]{:S(2)}, u32[]{:S(2)}) collective-permute-start(f32[136,128]{1,0:T(8,128)S(1)} %pad_maximum_fusion.1), channel_id=1, source_target_pairs={{0,3},{1,0},{2,1},{3,2},{4,7},{5,4},{6,5},{7,6},{8,11},{9,8},{10,9... | collective-permute-start | bytes 208904 | tf_op jit(solution)/shard_map/ppermute | solution.py:448
where the time goes:
time: 202 us; the launch traced here: 201 us
  waiting for transfers between devices  123 us (61%)
  Pallas kernels  55.2 us (27%)
  starting transfers between devices  18.4 us (9%)
  local copies, waits for them, and re-layouts  4.42 us (2%)
    all_to_all x1, waiting for transfers between devices, body(): lax.all_to_all(pieces, ('rows', 'cols'), split_axis=0, concat_axis=0, til...  93.1 us
    ppermute x6, waiting for transfers between devices, summed(): value = value + lax.ppermute(value, axis, pairs)  29.7 us
    pallas_call x1, Pallas kernels, ordered(): pl.pallas_call(order_kernel, grid=(rows // chunk,), in_specs=[pl.BlockSpe...  14.8 us
    pallas_call x2, Pallas kernels, three_rotations(): pl.pallas_call(rotation_kernel, out_shape=jax.ShapeDtypeStruct((3, 2 * wi...  11.6 us
    ppermute x4, starting transfers between devices, from_behind(): return lax.ppermute(value, axis, pairs)  7.41 us
    pallas_call x1, Pallas kernels, local_gram(): pl.pallas_call(gram_kernel, grid=(rows // chunk,), in_specs=[pl.BlockSpec...  7.23 us
    all_to_all x1, starting transfers between devices, body(): lax.all_to_all(pieces, ('rows', 'cols'), split_axis=0, concat_axis=0, til...  7.15 us
    pallas_call x1, Pallas kernels, finish(): pl.pallas_call(finish_kernel, grid=(rows // chunk,), in_specs=[pl.BlockSp...  5.2 us
  transfers between devices with their start and end apart: 11, of which 7 were waited for; matrix products, arithmetic and copies ran while one was open for 0% of the time, Pallas kernels for 21%

commit v1 on v0

v1 whole, which is shorter than its diff:
```python
import jax
import jax.numpy as jnp
from jax import lax
from jax.experimental import pallas as pl
from jax.experimental.pallas import tpu as pltpu
from jax.sharding import PartitionSpec as P

STEPS = 2
NS_STEPS = 6
SLOTS = 4
MIB = 1024 * 1024

F32 = jnp.float32
BF16 = jnp.bfloat16
NN = (((1,), (0,)), ((), ()))
NT = (((1,), (1,)), ((), ()))
TN = (((0,), (0,)), ((), ()))


def pair_slots(chosen):
    partner = 2 - chosen
    low = jnp.where(partner == 0, 1, 0)
    high = jnp.where(partner == 2, 1, 2)
    return partner, low, high


def params(mib, flops=0, moved=0):
    return dict(
        compiler_params=pltpu.CompilerParams(vmem_limit_bytes=mib * MIB),
        cost_estimate=pl.CostEstimate(flops=int(flops), bytes_accessed=int(moved), transcendentals=0),
    )


def halves(value):
    high = value.astype(BF16)
    return high, (value - high.astype(F32)).astype(BF16)


def mul(a, b, dims):
    return lax.dot_general(a, b, dims, preferred_element_type=F32)


def dot_split(a, b, dims):
    a_high, a_low = halves(a)
    b_high, b_low = halves(b)
    return mul(a_high, b_high, dims) + (mul(a_high, b_low, dims) + mul(a_low, b_high, dims))


def dot_full(a, b, dims=NN):
    return lax.dot_general(a, b, dims, precision=lax.Precision.HIGHEST, preferred_element_type=F32)


def identity(size):
    return lax.broadcasted_iota(jnp.int32, (size, size), 0) == lax.broadcasted_iota(jnp.int32, (size, size), 1)


LANES = 128
WAYS = 8


def block_rows(refs, slot):
    width = refs[0].shape[0] // SLOTS
    return jnp.concatenate([ref[pl.ds(slot, width, SLOTS), :] for ref in refs], axis=1)


def lane_specs(columns):
    return [pl.BlockSpec((columns, LANES), lambda k, way=way: (0, WAYS * k + way)) for way in range(WAYS)]


def at(ref, row, column, width):
    rows = pl.ds(pl.multiple_of(row * width, width), width)
    columns = pl.ds(pl.multiple_of(column * width, width), width)
    return ref[rows, columns]


def spread_kernel(tracks_ref, pieces_ref, came_ref, ready_ref, in_sems, out_sems):
    row_devices, frames, _, rows = came_ref.shape
    loads = [
        pltpu.make_async_copy(tracks_ref.at[:, :, pl.ds(r * rows, rows)], came_ref.at[r], in_sems.at[r])
        for r in range(row_devices)
    ]
    stores = [
        pltpu.make_async_copy(ready_ref.at[r], pieces_ref.at[r], out_sems.at[r]) for r in range(row_devices)
    ]
    for load in loads:
        load.start()
    for r in range(row_devices):
        loads[r].wait()
        for component in range(2):
            plane = came_ref[r, :, component, :]
            for group in range(frames // 8):
                for half in range(2):
                    ready_ref[r, 2 * component + half, 4 * group:4 * group + 4, :] = plane[
                        8 * group + 4 * half:8 * group + 4 * half + 4, :]
        stores[r].start()
    for store in stores:
        store.wait()


def spread(tracks, row_devices):
    frames, _, pixels = tracks.shape
    rows = pixels // row_devices
    shape = (row_devices, 4, frames // 2, rows)
    return pl.pallas_call(
        spread_kernel,
        in_specs=[pl.BlockSpec(memory_space=pl.ANY)],
        out_specs=pl.BlockSpec(memory_space=pl.ANY),
        out_shape=jax.ShapeDtypeStruct(shape, F32),
        scratch_shapes=[
            pltpu.VMEM((row_devices, frames, 2, rows), F32),
            pltpu.VMEM(shape, F32),
            pltpu.SemaphoreType.DMA((row_devices,)),
            pltpu.SemaphoreType.DMA((row_devices,)),
        ],
        name="spread",
        **params(48, 0, 8 * tracks.size),
    )(tracks)


def coupling_kernel(chosen_ref, *refs):
    held_refs, (sums_ref, last_ref, products_ref, squares_ref) = refs[:WAYS], refs[WAYS:]
    step = pl.program_id(0)
    width = sums_ref.shape[1]
    partner, first, second = pair_slots(chosen_ref[0])

    @pl.when(step == 0)
    def _():
        products_ref[...] = jnp.zeros_like(products_ref)
        squares_ref[...] = jnp.zeros_like(squares_ref)

    for index, slots in enumerate(((partner, SLOTS - 1), (first, second))):
        both = []
        for side, slot in enumerate(slots):
            block = block_rows(held_refs, slot)
            if index == 0:
                last_ref[side * width:(side + 1) * width, :] = block
            squared = block * block
            folded = squared[:, :LANES]
            for way in range(1, WAYS):
                folded += squared[:, way * LANES:(way + 1) * LANES]
            squares_ref[2 * index + side] += folded
            both.append(jnp.concatenate(halves(block), axis=0))
        products_ref[index] += mul(both[0], both[1], NT)

    @pl.when(step == pl.num_programs(0) - 1)
    def _():
        for index in range(2):
            product = products_ref[index]
            top = product[:width, :width] + (product[:width, width:] + product[width:, :width])
            sums_ref[index * width:(index + 1) * width, :] = top + product[width:, width:]
        rows = [jnp.sum(squares_ref[slot].T, axis=0, keepdims=True) for slot in range(SLOTS)]
        sums_ref[2 * width:, :] = jnp.concatenate(rows + [jnp.zeros((4, width), F32)], axis=0)


def couplings(chosen, held):
    columns, rows = held.shape
    width = columns // SLOTS
    chunk = WAYS * LANES
    return pl.pallas_call(
        coupling_kernel,
        grid=(rows // chunk,),
        in_specs=[pl.BlockSpec(memory_space=pltpu.SMEM)] + lane_specs(columns),
        out_specs=[
            pl.BlockSpec((2 * width + 8, width), lambda k: (0, 0)),
            pl.BlockSpec((2 * width, chunk), lambda k: (0, k)),
        ],
        out_shape=[
            jax.ShapeDtypeStruct((2 * width + 8, width), F32),
            jax.ShapeDtypeStruct((2 * width, rows), F32),
        ],
        scratch_shapes=[
            pltpu.VMEM((2, 2 * width, 2 * width), F32),
            pltpu.VMEM((SLOTS, width, LANES), F32),
        ],
        name="couplings",
        **params(24, 16 * width * width * rows, 6 * held.size),
    )(chosen, *[held] * WAYS)


def gram_kernel(*refs):
    held_refs, (_, gram_ref, split_ref, cross_ref) = refs[:WAYS], refs[WAYS:]
    step = pl.program_id(0)
    columns = gram_ref.shape[0]
    high, low = halves(jnp.concatenate([block_rows(held_refs, b) for b in range(SLOTS)], axis=0))
    split_ref[:columns, :] = high
    split_ref[columns:, :] = low

    @pl.when(step == 0)
    def _():
        gram_ref[...] = mul(high, high, NT)
        cross_ref[...] = mul(high, low, NT)

    @pl.when(step > 0)
    def _():
        gram_ref[...] += mul(high, high, NT)
        cross_ref[...] += mul(high, low, NT)

    @pl.when(step == pl.num_programs(0) - 1)
    def _():
        cross = cross_ref[...]
        gram_ref[...] += cross + cross.T


def local_gram(held, after):
    columns, rows = held.shape
    chunk = WAYS * LANES
    return pl.pallas_call(
        gram_kernel,
        grid=(rows // chunk,),
        in_specs=lane_specs(columns) + [pl.BlockSpec(memory_space=pl.ANY)],
        out_specs=[
            pl.BlockSpec((columns, columns), lambda k: (0, 0)),
            pl.BlockSpec((2 * columns, chunk), lambda k: (0, k)),
        ],
        out_shape=[
            jax.ShapeDtypeStruct((columns, columns), F32),
            jax.ShapeDtypeStruct((2 * columns, rows), BF16),
        ],
        scratch_shapes=[pltpu.VMEM((columns, columns), F32)],
        name="gram",
        **params(32, 4 * columns * columns * rows, 8 * held.size),
    )(*[held] * WAYS, after)


def cross_kernel(chosen_ref, split_ref, came_ref, _, cross_ref, own_ref):
    width = came_ref.shape[0] // 2
    columns = split_ref.shape[0] // 2
    partner, first, second = pair_slots(chosen_ref[0])
    in_last = 2 - chosen_ref[1] == partner
    members = (jnp.where(in_last, partner, first), jnp.where(in_last, SLOTS - 1, second))
    here_high, here_low = [
        jnp.concatenate(
            [split_ref[pl.ds(pl.multiple_of(start + m * width, width), width), :] for m in members], axis=0)
        for start in (0, columns)
    ]
    came_high, came_low = halves(came_ref[...])
    cross_ref[...] = mul(here_high, came_high, NT) + (mul(here_high, came_low, NT) + mul(here_low, came_high, NT))
    twice = mul(came_high, came_low, NT)
    own_ref[...] = mul(came_high, came_high, NT) + (twice + twice.T)


def cross_gram(chosen, split, came, after):
    pair, rows = came.shape
    vmem = pl.BlockSpec(memory_space=pltpu.VMEM)
    square = jax.ShapeDtypeStruct((pair, pair), F32)
    return pl.pallas_call(
        cross_kernel,
        in_specs=[pl.BlockSpec(memory_space=pltpu.SMEM), vmem, vmem, pl.BlockSpec(memory_space=pl.ANY)],
        out_specs=[vmem, vmem],
        out_shape=[square, square],
        name="cross_gram",
        **params(24, 10 * pair * pair * rows, 8 * came.size),
    )(chosen, split, came, after)


def rotations(grams):
    width = grams[0][0].shape[0]
    eye = identity(width).astype(F32)
    couplings, scales, squares, products = [], [], [], []
    for block, row_sums, column_sums in grams:
        spread_sums = jnp.broadcast_to(row_sums, (width, width)).T
        coupling = block / (spread_sums + column_sums)
        total = 1.0 + jnp.sum(coupling * coupling)
        couplings.append(coupling)
        for dims in (NT, TN):
            scales.append(1.0 / jnp.sqrt(total))
            squares.append((eye + dot_full(coupling, coupling, dims)) / total)
    for count in range(NS_STEPS):
        factors = [1.5 * eye - 0.5 * square for square in squares]
        if count == 0:
            products = [scale * factor for scale, factor in zip(scales, factors)]
        else:
            products = [dot_full(product, factor) for product, factor in zip(products, factors)]
        if count + 1 < NS_STEPS:
            squares = [dot_full(square, factor) for square, factor in zip(squares, factors)]
            squares = [dot_full(square, factor) for square, factor in zip(squares, factors)]
    results = []
    for index, coupling in enumerate(couplings):
        across = dot_full(products[2 * index], coupling)
        results.append((products[2 * index], across, -across.T, products[2 * index + 1]))
    return results


def rotation_kernel(sums_ref, came_ref, *refs):
    rotation_ref = refs[-1]
    width = sums_ref.shape[1]
    sums = sums_ref[2 * width:, :]
    came = came_ref[width:, :]
    grams = [
        (sums_ref[:width, :], sums[0:1], sums[1:2]),
        (sums_ref[width:2 * width, :], sums[2:3], sums[3:4]),
        (came_ref[:width, :], came[0:1], came[1:2]),
    ]
    for index, (top, right, bottom, end) in enumerate(rotations(grams)):
        rotation_ref[index, :width, :width] = top
        rotation_ref[index, :width, width:] = right
        rotation_ref[index, width:, :width] = bottom
        rotation_ref[index, width:, width:] = end


def three_rotations(sums, came, *after):
    width = sums.shape[1]
    vmem = pl.BlockSpec(memory_space=pltpu.VMEM)
    return pl.pallas_call(
        rotation_kernel,
        in_specs=[vmem, vmem] + [pl.BlockSpec(memory_space=pl.ANY)] * len(after),
        out_specs=vmem,
        out_shape=jax.ShapeDtypeStruct((3, 2 * width, 2 * width), F32),
        name="rotations",
        **params(16, 200 * 6 * width**3, 16 * width * width),
    )(sums, came, *after)


def second_kernel(chosen_ref, gram_ref, cross_ref, own_ref, rotation_ref, sums_ref):
    width = sums_ref.shape[1]
    partner, first, second = pair_slots(chosen_ref[0])
    meets, low, high = pair_slots(chosen_ref[1])

    def place(slot):
        in_last = slot == partner
        members = (jnp.where(in_last, partner, first), jnp.where(in_last, SLOTS - 1, second))
        columns = jnp.where(jnp.logical_or(in_last, slot == first), 0, 1)
        turn = rotation_ref[jnp.where(in_last, 0, 1), :, pl.ds(pl.multiple_of(columns * width, width), width)]
        return members, turn

    def between(rows, columns):
        return jnp.concatenate(
            [jnp.concatenate([at(gram_ref, r, c, width) for c in columns], axis=1) for r in rows], axis=0)

    (meets_in, meets_turn), (low_in, low_turn), (high_in, high_turn) = place(meets), place(low), place(high)
    came_turn = rotation_ref[2, :, width:]
    sums_ref[:width, :] = dot_split(meets_turn, dot_split(cross_ref[...], came_turn, NN), TN)
    sums_ref[width:2 * width, :] = dot_split(low_turn, dot_split(between(low_in, high_in), high_turn, NN), TN)

    def squares(gram, turn):
        return jnp.sum(turn * dot_split(gram, turn, NN), axis=0, keepdims=True)

    rows = [
        squares(between(meets_in, meets_in), meets_turn),
        squares(own_ref[...], came_turn),
        squares(between(low_in, low_in), low_turn),
        squares(between(high_in, high_in), high_turn),
        jnp.zeros((4, width), F32),
    ]
    sums_ref[2 * width:, :] = jnp.concatenate(rows, axis=0)


def second_sums(chosen, gram, cross, own, turns):
    width = gram.shape[0] // SLOTS
    vmem = pl.BlockSpec(memory_space=pltpu.VMEM)
    return pl.pallas_call(
        second_kernel,
        in_specs=[pl.BlockSpec(memory_space=pltpu.SMEM)] + [vmem] * 4,
        out_specs=vmem,
        out_shape=jax.ShapeDtypeStruct((2 * width + 8, width), F32),
        name="second_sums",
        **params(16, 6 * 32 * width**3, 16 * gram.size),
    )(chosen, gram, cross, own, turns)


def picks(order_ref, rows):
    order = order_ref[...]
    return jnp.where(lax.broadcasted_iota(jnp.int32, (rows, order.shape[1]), 0) == order, 1.0, 0.0).astype(BF16)


def order_kernel(order_ref, split_ref, *refs):
    matrix_ref = refs[-1]
    rows = split_ref.shape[1]
    width = matrix_ref.shape[2]
    columns = SLOTS * width
    both = mul(split_ref[...], picks(order_ref, rows), NN)
    both = both[:columns] + both[columns:]
    for block in range(SLOTS):
        matrix_ref[block] = both[block * width:(block + 1) * width].T


def ordered(order, split, after, tiles, into=None):
    columns, rows = split.shape[0] // 2, split.shape[1]
    width = columns // SLOTS
    chunk = 2 * width
    start, stop = tiles
    extra = (after,) if into is None else (after, into)
    return pl.pallas_call(
        order_kernel,
        grid=(stop - start,),
        in_specs=[
            pl.BlockSpec((1, chunk), lambda k: (0, k + start)),
            pl.BlockSpec((2 * columns, rows), lambda k: (0, 0)),
        ] + [pl.BlockSpec(memory_space=pl.ANY)] * len(extra),
        out_specs=pl.BlockSpec((SLOTS, chunk, width), lambda k: (0, k + start, 0)),
        out_shape=jax.ShapeDtypeStruct((SLOTS, rows, width), F32),
        input_output_aliases={} if into is None else {3: 0},
        name="row_order",
        **params(32, 4 * columns * rows * chunk * (stop - start), 8 * columns * rows),
    )(order, split, *extra)


def turn_kernel(chosen_ref, matrix_ref, rotation_ref, _, turned_ref, meets_ref):
    width = matrix_ref.shape[2]
    partner, first, second = pair_slots(chosen_ref[0])
    for index, (one, two) in enumerate(((partner, SLOTS - 1), (first, second))):
        pair = jnp.concatenate([matrix_ref[one], matrix_ref[two]], axis=1)
        turned = dot_split(pair, rotation_ref[index], NN)
        turned_ref[one] = turned[:, :width]
        turned_ref[two] = turned[:, width:]
    meets_ref[...] = turned_ref[2 - chosen_ref[1]]


def turn(chosen, matrix, turns, after):
    _, rows, width = matrix.shape
    chunk = rows // 2
    return pl.pallas_call(
        turn_kernel,
        grid=(rows // chunk,),
        in_specs=[
            pl.BlockSpec(memory_space=pltpu.SMEM),
            pl.BlockSpec((SLOTS, chunk, width), lambda k: (0, k, 0)),
            pl.BlockSpec(turns.shape, lambda k: (0, 0, 0)),
            pl.BlockSpec(memory_space=pl.ANY),
        ],
        out_specs=[
            pl.BlockSpec((SLOTS, chunk, width), lambda k: (0, k, 0)),
            pl.BlockSpec((chunk, width), lambda k: (k, 0)),
        ],
        out_shape=[jax.ShapeDtypeStruct(matrix.shape, F32), jax.ShapeDtypeStruct((rows, width), F32)],
        name="first_turn",
        **params(32, 24 * rows * width * width, 9 * matrix.size),
    )(chosen, matrix, turns, after)


def moved_kernel(order_ref, came_ref, rotation_ref, _, block_ref, split_ref):
    width = block_ref.shape[1]
    rows = came_ref.shape[1]

    @pl.when(pl.program_id(0) == 0)
    def _():
        high, low = halves(dot_split(rotation_ref[2, :, width:], came_ref[...], TN))
        split_ref[:width, :] = high
        split_ref[width:, :] = low

    both = mul(split_ref[...], picks(order_ref, rows), NN)
    block_ref[...] = (both[:width] + both[width:]).T


def moved_block(order, came, turns, after):
    pair, rows = came.shape
    width = pair // 2
    chunk = pair
    return pl.pallas_call(
        moved_kernel,
        grid=(rows // chunk,),
        in_specs=[
            pl.BlockSpec((1, chunk), lambda k: (0, k)),
            pl.BlockSpec((pair, rows), lambda k: (0, 0)),
            pl.BlockSpec(turns.shape, lambda k: (0, 0, 0)),
            pl.BlockSpec(memory_space=pl.ANY),
        ],
        out_specs=pl.BlockSpec((chunk, width), lambda k: (k, 0)),
        out_shape=jax.ShapeDtypeStruct((rows, width), F32),
        scratch_shapes=[pltpu.VMEM((pair, rows), BF16)],
        name="moved_block",
        **params(32, 4 * width * rows * rows, 8 * came.size),
    )(order, came, turns, after)


PARTS = 4


def finish_kernel(chosen_ref, turned_ref, moved_ref, behind_ref, rotation_ref, out_ref, ready_ref, sems):
    rows, width = moved_ref.shape
    meets, low, high = pair_slots(chosen_ref[1])
    chunk = rows // PARTS
    stores = []
    for part in range(PARTS):
        here = pl.ds(part * chunk, chunk)

        def put(slot, value, here=here):
            ready_ref[here, pl.ds(pl.multiple_of(slot * width, width), width)] = value

        pair = dot_split(jnp.concatenate([turned_ref[low, here], turned_ref[high, here]], axis=1), rotation_ref[1], NN)
        put(low, pair[:, :width])
        put(high, pair[:, width:])
        put(meets, dot_split(
            jnp.concatenate([turned_ref[meets, here], moved_ref[here]], axis=1), rotation_ref[0, :, :width], NN))
        put(SLOTS - 1, dot_split(
            jnp.concatenate([behind_ref[here], turned_ref[SLOTS - 1, here]], axis=1), rotation_ref[2, :, width:], NN))
        stores.append(pltpu.make_async_copy(ready_ref.at[here], out_ref.at[here], sems.at[part]))
        stores[-1].start()
    for store in stores:
        store.wait()


def finish(chosen, turned, moved, behind, turns):
    _, rows, width = turned.shape
    vmem = pl.BlockSpec(memory_space=pltpu.VMEM)
    return pl.pallas_call(
        finish_kernel,
        in_specs=[pl.BlockSpec(memory_space=pltpu.SMEM)] + [vmem] * 4,
        out_specs=pl.BlockSpec(memory_space=pl.ANY),
        out_shape=jax.ShapeDtypeStruct((rows, SLOTS * width), F32),
        scratch_shapes=[pltpu.VMEM((rows, SLOTS * width), F32), pltpu.SemaphoreType.DMA((PARTS,))],
        name="second_turn",
        **params(32, 24 * rows * width * width, 10 * turned.size),
    )(chosen, turned, moved, behind, turns)


def add_kernel(one_ref, two_ref, *refs):
    total_ref, last_ref = refs[-2:]
    width = one_ref.shape[1]
    total = one_ref[...] + two_ref[...]
    total_ref[...] = total
    last_ref[:width] = total[:width]
    last_ref[width:] = total[2 * width:]


def added(one, two, after):
    height, width = one.shape
    vmem = pl.BlockSpec(memory_space=pltpu.VMEM)
    return pl.pallas_call(
        add_kernel,
        in_specs=[vmem, vmem] + [pl.BlockSpec(memory_space=pl.ANY)] * len(after),
        out_specs=[vmem, vmem],
        out_shape=[jax.ShapeDtypeStruct(one.shape, F32), jax.ShapeDtypeStruct((height - width, width), F32)],
        name="add",
        **params(8, one.size, 16 * one.size),
    )(one, two, *after)


def from_behind(value, axis, steps):
    count = lax.axis_size(axis)
    pairs = [(source, (source + steps) % count) for source in range(count)]
    return lax.ppermute(value, axis, pairs)


def summed(value, axis, beside):
    count = lax.axis_size(axis)
    width = value.shape[1]
    last = None
    distance = 1
    while distance < count:
        if count & (count - 1):
            value, distance = lax.psum(value, axis), count
            break
        got = lax.ppermute(value, axis, [(source, source ^ distance) for source in range(count)])
        after = beside.pop(0)(value) if beside else ()
        value, last = added(value, got, after)
        distance *= 2
    for work in beside:
        work(value)
    if last is None:
        last = jnp.concatenate([value[:width], value[2 * width:]], axis=0)
    return value, last


def body(tracks, pixel_order, pairing):
    frames_dev, _, pixel_total = tracks.shape
    row_devices = lax.axis_size("rows")
    row_count = pixel_total // row_devices
    pieces = spread(tracks, row_devices).reshape(row_devices * 4, frames_dev // 2, row_count)
    arrived = lax.all_to_all(pieces, ("rows", "cols"), split_axis=0, concat_axis=0, tiled=True)
    held = arrived.reshape(-1, row_count)
    order = (pixel_order - lax.axis_index("rows") * row_count).reshape(1, row_count)
    chosen = lax.dynamic_index_in_dim(pairing, lax.axis_index("cols"), axis=1, keepdims=False)
    tiles = row_count // (held.shape[0] // 2)
    kept = {}

    def gram_work(after):
        kept["gram"], kept["split"] = local_gram(held, after)
        return (kept["gram"],)

    def order_first(after):
        kept["matrix"] = ordered(order, kept["split"], after, (0, tiles * 3 // 8))
        return (kept["matrix"],)

    def order_rest(after):
        kept["matrix"] = ordered(order, kept["split"], after, (tiles * 3 // 8, tiles), kept["matrix"])
        return (kept["matrix"],)

    def turn_work(after):
        kept["turned"], meets = turn(chosen, kept["matrix"], kept["turns"], after)
        kept["behind"] = from_behind(meets, "cols", -1)
        return (meets,)

    def moved_work(after):
        kept["moved"] = moved_block(order, came, kept["turns"], after)
        return (kept["moved"],)

    sums, last = couplings(chosen, held)
    came = from_behind(last, "cols", 1)
    sums, last_sums = summed(sums, "rows", [gram_work, order_first, order_rest])
    came_sums = from_behind(last_sums, "cols", 1)
    cross, own = cross_gram(chosen, kept["split"], came, sums)
    kept["turns"] = three_rotations(sums, came_sums, cross)

    sums = second_sums(chosen, kept["gram"], cross, own, kept["turns"])
    sums, last_sums = summed(sums, "rows", [turn_work, moved_work])
    behind_sums = from_behind(last_sums, "cols", -1)
    return finish(chosen, kept["turned"], kept["moved"], kept["behind"], three_rotations(sums, behind_sums))


def solution(mesh):
    placed = (P(("rows", "cols"), None, None), P("rows"), P())
    return jax.shard_map(
        body, mesh=mesh, in_specs=placed, out_specs=P("rows", "cols"), check_vma=False
    )
```

time: 202 us -> 184 us (0.911)
  waiting for transfers between devices: 123 us -> 110 us
  local copies, waits for them, and re-layouts: 4.42 us -> 2.2 us
    ppermute x6, waiting for transfers between devices: 29.7 us -> 14 us  [summed(): lax.ppermute(value, axis, [(source, source ^ distance) for source in rang...]
    ppermute x4, waiting for transfers between devices: 0.01 us -> 2.36 us  [from_behind(): return lax.ppermute(value, axis, pairs)]
    unnamed x8 -> x6, local copies, waits for them, and re-layouts: 4.22 us -> 2.02 us
    pallas_call x7 -> x15, Pallas kernels: 44.5 us -> 44.7 us  [the longest x2 11.6 us: three_rotations(): pl.pallas_call(rotation_kernel, in_specs=[vmem, vmem] + [pl.BlockSpec(mem...]
  transfers between devices with their start and end apart: 11 -> 11, of which waited for: 7 -> 6; matrix products, arithmetic and copies ran while one was open for 0% -> 0% of each run, Pallas kernels for 21% -> 18%
where the time goes in v1:
time: 184 us
  waiting for transfers between devices  110 us (60%)
  Pallas kernels  54.7 us (30%)
  starting transfers between devices  17.1 us (9%)
  local copies, waits for them, and re-layouts  2.2 us (1%)
    all_to_all x1, waiting for transfers between devices, body(): lax.all_to_all(pieces, ('rows', 'cols'), split_axis=0, concat_axis=0, til...  93.1 us
    ppermute x6, waiting for transfers between devices, summed(): lax.ppermute(value, axis, [(source, source ^ distance) for source in rang...  14 us
    pallas_call x2, Pallas kernels, three_rotations(): pl.pallas_call(rotation_kernel, in_specs=[vmem, vmem] + [pl.BlockSpec(mem...  11.6 us
    pallas_call x2, Pallas kernels, ordered(): pl.pallas_call(order_kernel, grid=(stop - start,), in_specs=[pl.BlockSpec...  10.9 us
    all_to_all x1, starting transfers between devices, body(): lax.all_to_all(pieces, ('rows', 'cols'), split_axis=0, concat_axis=0, til...  7.15 us
    pallas_call x1, Pallas kernels, local_gram(): pl.pallas_call(gram_kernel, grid=(rows // chunk,), in_specs=lane_specs(co...  6.07 us
    ppermute x4, starting transfers between devices, from_behind(): return lax.ppermute(value, axis, pairs)  6.02 us
    pallas_call x1, Pallas kernels, moved_block(): pl.pallas_call(moved_kernel, grid=(rows // chunk,), in_specs=[pl.BlockSpe...  4.96 us
  transfers between devices with their start and end apart: 11, of which 6 were waited for; matrix products, arithmetic and copies ran while one was open for 0% of the time, Pallas kernels for 18%

profile of v1, /device:TPU:1, one launch (start us, length us, event | category | flops | bytes accessed | tf_op | source)
XLA Modules:
  0.0 183.9 jit_solution(6371759328883953176)
XLA Ops:
  0.0 0.0 copy-start
  0.0 2.5 %spread.1 = f32[8,4,16,2048]{3,2,1,0:T(8,128)S(1)} custom-call(f32[32,2,16384]{2,1,0:T(2,128)} %tracks_ref.1), custom_call_target="tpu_custom_call" | custom-call | bytes 8388608 | tf_op jit(solution)/shard_map/spread/pallas_call | solution.py:104
  2.5 0.0 copy-start.1
  2.5 2.0 %copy-done.1 = f32[8,4,16,2048]{3,2,1,0:T(8,128)} copy-done((f32[8,4,16,2048]{3,2,1,0:T(8,128)}, f32[8,4,16,2048]{3,2,1,0:T(8,128)S(1)}, u32[]{:S(2)}) %copy-start.1) | copy-done | bytes 4194328
  4.5 7.2 %all-to-all-start = ((f32[32,16,2048]{2,1,0:T(8,128)}), f32[32,16,2048]{2,1,0:T(8,128)}, u32[]{:S(2)}, u32[]{:S(2)}) async-start(f32[32,16,2048]{2,1,0:T(8,128)} %bitcast.3), calls=%async_computation | async-start | bytes 8388608 | tf_op jit(solution)/shard_map/all_to_all | solution.py:560
  11.7 0.0 copy-done
  11.7 0.2 dynamic-slice_reduce_fusion.chosen_ref
  11.8 93.1 %all-to-all-done = f32[32,16,2048]{2,1,0:T(8,128)} async-done(((f32[32,16,2048]{2,1,0:T(8,128)}), f32[32,16,2048]{2,1,0:T(8,128)}, u32[]{:S(2)}, u32[]{:S(2)}) %all-to-all-start) | async-done | bytes 4194336 | tf_op jit(solution)/shard_map/all_to_all | solution.py:560
  105.0 0.0 copy-start.2
  105.0 4.2 %couplings.1 = (f32[264,128]{1,0:T(8,128)S(1)}, f32[256,2048]{1,0:T(8,128)}) custom-call(s32[2]{0:T(128)S(1)} %dynamic-slice_reduce_fusion.chosen_ref, f32[512,2048]{1,0:T(8,128)} %bitcast.2.refs_0_.refs_1_.refs_2_.refs_3_.refs_4_.refs_5_.refs_6_.refs_7_, f32[512,2048]{1,0:T(8,128)} %bitcast.2.refs_0_.refs_1_.refs_2_.refs_3_.refs_4_.refs_5_.refs_6_.refs_7_, ...), custom_call_target="tpu_custom_call" | custom-call | flops 536870912 | bytes 6291456 | tf_op jit(solution)/shard_map/couplings/pallas_call | solution.py:159
  109.2 1.7 collective-permute-start.4
  111.0 0.0 copy-done.2
  111.0 1.4 collective-permute-start
  112.4 6.1 %gram.1 = (f32[512,512]{1,0:T(8,128)S(1)}, bf16[1024,2048]{1,0:T(8,128)(2,1)S(1)}) custom-call(f32[512,2048]{1,0:T(8,128)} %bitcast.2.refs_0_.refs_1_.refs_2_.refs_3_.refs_4_.refs_5_.refs_6_.refs_7_, f32[512,2048]{1,0:T(8,128)} %bitcast.2.refs_0_.refs_1_.refs_2_.refs_3_.refs_4_.refs_5_.refs_6_.refs_7_, ...), custom_call_target="tpu_custom_call" | custom-call | flops 2147483648 | bytes 8388608 | tf_op jit(solution)/shard_map/gram/pallas_call | solution.py:207
  118.5 0.0 collective-permute-done.two_ref
  118.5 0.6 add.12
  119.1 0.0 collective-permute-start.1
  119.1 4.1 %row_order.2.refs_0_.refs_1_ = f32[4,2048,128]{2,1,0:T(8,128)S(1)} custom-call(s32[1,2048]{1,0:T(1,128)S(1)} %bitcast.4, bf16[1024,2048]{1,0:T(8,128)(2,1)S(1)} %get-tuple-element.22.split_ref, f32[264,128]{1,0:T(8,128)S(1)} %get-tuple-element.24.refs_0_.one_ref), custom_call_target="tpu_custom_call" | custom-call | flops 3221225472 | bytes 8388608 | tf_op jit(solution)/shard_map/row_order/pallas_call | solution.py:383
  123.2 1.0 collective-permute-done.1.two_ref
  124.2 0.6 add.13
  124.9 0.8 collective-permute-start.2
  125.6 6.8 %row_order.3.refs_0_.matrix_ref = f32[4,2048,128]{2,1,0:T(8,128)S(1)} custom-call(s32[1,2048]{1,0:T(1,128)S(1)} %bitcast.5, bf16[1024,2048]{1,0:T(8,128)(2,1)S(1)} %get-tuple-element.22.split_ref, f32[264,128]{1,0:T(8,128)S(1)} %get-tuple-element.25.refs_0_.one_ref, f32[4,2048,128]{2,1,0:T(8,128)S(1)} %row_order.2.refs_0_.refs_1_), custom_call_target="tpu_custom_call", output_to_operand_aliasing={{}: (3, {})} | custom-call | flops 5368709120 | bytes 8388608 | tf_op jit(solution)/shard_map/row_order/pallas_call | solution.py:383
  132.4 1.7 collective-permute-done.2.two_ref
  134.2 0.2 collective-permute-start.3
  134.4 0.0 collective-permute-done.4.came_ref
  134.4 2.2 %cross_gram.1 = (f32[256,256]{1,0:T(8,128)S(1)}, f32[256,256]{1,0:T(8,128)S(1)}) custom-call(s32[2]{0:T(128)S(1)} %dynamic-slice_reduce_fusion.chosen_ref, bf16[1024,2048]{1,0:T(8,128)(2,1)S(1)} %get-tuple-element.22.split_ref, f32[256,2048]{1,0:T(8,128)S(1)} %collective-permute-done.4.came_ref, f32[264,128]{1,0:T(8,128)S(1)} %get-tuple-element.26._.sums_ref), custom_call_target="tpu_custom_call" | custom-call | flops 1342177280 | bytes 4194304 | tf_op jit(solution)/shard_map/cross_gram/pallas_call | solution.py:246
  136.6 0.0 collective-permute-done.3.came_ref
  136.6 5.8 %rotations.2.rotation_ref = f32[3,256,256]{2,1,0:T(8,128)S(1)} custom-call(f32[264,128]{1,0:T(8,128)S(1)} %get-tuple-element.26._.sums_ref, f32[136,128]{1,0:T(8,128)S(1)} %collective-permute-done.3.came_ref, f32[256,256]{1,0:T(8,128)S(1)} %get-tuple-element.29.refs_0_.cross_ref), custom_call_target="tpu_custom_call" | custom-call | flops 2516582400 | bytes 262144 | tf_op jit(solution)/shard_map/rotations/pallas_call | solution.py:304
  142.5 1.8 second_sums.1._.one_ref
  144.3 3.3 %first_turn.1 = (f32[4,2048,128]{2,1,0:T(8,128)S(1)}, f32[2048,128]{1,0:T(8,128)S(1)}) custom-call(s32[2]{0:T(128)S(1)} %dynamic-slice_reduce_fusion.chosen_ref, f32[4,2048,128]{2,1,0:T(8,128)S(1)} %row_order.3.refs_0_.matrix_ref, f32[3,256,256]{2,1,0:T(8,128)S(1)} %rotations.2.rotation_ref, f32[264,128]{1,0:T(8,128)S(1)} %second_sums.1._.one_ref), custom_call_target="tpu_custom_call" | custom-call | flops 805306368 | bytes 9437184 | tf_op jit(solution)/shard_map/first_turn/pallas_call | solution.py:412
  147.6 2.0 %collective-permute-start.6 = (f32[2048,128]{1,0:T(8,128)S(1)}, f32[2048,128]{1,0:T(8,128)S(1)}, u32[]{:S(2)}, u32[]{:S(2)}) collective-permute-start(f32[2048,128]{1,0:T(8,128)S(1)} %get-tuple-element.32.refs_0_), channel_id=1, source_target_pairs={{0,3},{1,0},{2,1},{3,2},{4,7},{5,4},{6,5},{7,6},{8,11},{9,8},{10,9... | collective-permute-start | bytes 3145736 | tf_op jit(solution)/shard_map/ppermute | solution.py:532
  149.6 0.3 collective-permute-start.5
  149.9 4.7 %collective-permute-done.5.two_ref = f32[264,128]{1,0:T(8,128)S(1)} collective-permute-done((f32[264,128]{1,0:T(8,128)S(1)}, f32[264,128]{1,0:T(8,128)S(1)}, u32[]{:S(2)}, u32[]{:S(2)}) %collective-permute-start.5) | collective-permute-done | bytes 135200 | tf_op jit(solution)/shard_map/ppermute | solution.py:544
  154.6 0.6 add.15
  155.3 0.0 collective-permute-start.7
  155.3 5.0 %moved_block.1.refs_0_.moved_ref = f32[2048,128]{1,0:T(8,128)S(1)} custom-call(s32[1,2048]{1,0:T(1,128)S(1)} %bitcast.6, f32[256,2048]{1,0:T(8,128)S(1)} %collective-permute-done.4.came_ref, f32[3,256,256]{2,1,0:T(8,128)S(1)} %rotations.2.rotation_ref, f32[264,128]{1,0:T(8,128)S(1)} %get-tuple-element.33._.one_ref), custom_call_target="tpu_custom_call" | custom-call | flops 2147483648 | bytes 4194304 | tf_op jit(solution)/shard_map/moved_block/pallas_call | solution.py:449
  160.2 0.0 collective-permute-done.7.two_ref
  160.2 0.7 add.16
  160.9 1.5 collective-permute-start.8
  162.4 6.6 %collective-permute-done.8.two_ref = f32[264,128]{1,0:T(8,128)S(1)} collective-permute-done((f32[264,128]{1,0:T(8,128)S(1)}, f32[264,128]{1,0:T(8,128)S(1)}, u32[]{:S(2)}, u32[]{:S(2)}) %collective-permute-start.8) | collective-permute-done | bytes 135200 | tf_op jit(solution)/shard_map/ppermute | solution.py:544
  169.0 2.0 %collective-permute-start.9 = (f32[136,128]{1,0:T(8,128)S(1)}, f32[136,128]{1,0:T(8,128)S(1)}, u32[]{:S(2)}, u32[]{:S(2)}) collective-permute-start(f32[136,128]{1,0:T(8,128)S(1)} %get-tuple-element.36), channel_id=1, source_target_pairs={{0,3},{1,0},{2,1},{3,2},{4,7},{5,4},{6,5},{7,6},{8,11},{9,8},{10,9... | collective-permute-start | bytes 208904 | tf_op jit(solution)/shard_map/ppermute | solution.py:532
  171.0 2.3 %collective-permute-done.9.came_ref = f32[136,128]{1,0:T(8,128)S(1)} collective-permute-done((f32[136,128]{1,0:T(8,128)S(1)}, f32[136,128]{1,0:T(8,128)S(1)}, u32[]{:S(2)}, u32[]{:S(2)}) %collective-permute-start.9) | collective-permute-done | bytes 69664 | tf_op jit(solution)/shard_map/ppermute | solution.py:532
  173.3 5.8 %rotations.3.rotation_ref = f32[3,256,256]{2,1,0:T(8,128)S(1)} custom-call(f32[264,128]{1,0:T(8,128)S(1)} %get-tuple-element.35.sums_ref, f32[136,128]{1,0:T(8,128)S(1)} %collective-permute-done.9.came_ref), custom_call_target="tpu_custom_call" | custom-call | flops 2516582400 | bytes 262144 | tf_op jit(solution)/shard_map/rotations/pallas_call | solution.py:304
  179.2 0.0 collective-permute-done.6.behind_ref
  179.2 4.6 %second_turn.1 = f32[2048,512]{1,0:T(8,128)} custom-call(s32[2]{0:T(128)S(1)} %dynamic-slice_reduce_fusion.chosen_ref, f32[4,2048,128]{2,1,0:T(8,128)S(1)} %get-tuple-element.31.turned_ref, f32[2048,128]{1,0:T(8,128)S(1)} %moved_block.1.refs_0_.moved_ref, f32[2048,128]{1,0:T(8,128)S(1)} %collective-permute-done.6.behind_ref, ...), custom_call_target="tpu_custom_call" | custom-call | flops 805306368 | bytes 10485760 | tf_op jit(solution)/shard_map/second_turn/pallas_call | solution.py:496
  (3 shorter events, 0.0 us)
Async XLA Ops:
  0.0 11.7 %copy-start = (s32[2,4]{1,0:T(2,128)S(1)}, s32[2,4]{1,0:T(2,128)}, u32[]{:S(2)}) copy-start(s32[2,4]{1,0:T(2,128)} %param.5) | copy-start | bytes 100
  2.5 2.0 %copy-start.1 = (f32[8,4,16,2048]{3,2,1,0:T(8,128)}, f32[8,4,16,2048]{3,2,1,0:T(8,128)S(1)}, u32[]{:S(2)}) copy-start(f32[8,4,16,2048]{3,2,1,0:T(8,128)S(1)} %spread.1) | copy-start | bytes 12582916
  4.5 100.5 %all-to-all-start = ((f32[32,16,2048]{2,1,0:T(8,128)}), f32[32,16,2048]{2,1,0:T(8,128)}, u32[]{:S(2)}, u32[]{:S(2)}) async-start(f32[32,16,2048]{2,1,0:T(8,128)} %bitcast.3), calls=%async_computation | async-start | bytes 8388608 | tf_op jit(solution)/shard_map/all_to_all | solution.py:560
  105.0 6.0 %copy-start.2 = (s32[2048]{0:T(1024)S(1)}, s32[2048]{0:T(1024)}, u32[]{:S(2)}) copy-start(s32[2048]{0:T(1024)} %param.4) | copy-start | bytes 24580
  109.2 25.2 %collective-permute-start.4 = (f32[256,2048]{1,0:T(8,128)}, f32[256,2048]{1,0:T(8,128)S(1)}, u32[]{:S(2)}, u32[]{:S(2)}) collective-permute-start(f32[256,2048]{1,0:T(8,128)} %get-tuple-element.28), channel_id=1, source_target_pairs={{0,1},{1,2},{2,3},{3,0},{4,5},{5,6},{6,7},{7,4},{8,9},{9,10},{10,1... | collective-permute-start | bytes 6291464 | tf_op jit(solution)/shard_map/ppermute | solution.py:532
  111.0 7.5 %collective-permute-start = (f32[264,128]{1,0:T(8,128)S(1)}, f32[264,128]{1,0:T(8,128)S(1)}, u32[]{:S(2)}, u32[]{:S(2)}) collective-permute-start(f32[264,128]{1,0:T(8,128)S(1)} %get-tuple-element.21.refs_8_.one_ref), channel_id=1, source_target_pairs={{0,4},{4,0},{8,12},{12,8},{16,20},{20,16},{24,28},{28,24},{1,5},{5... | collective-permute-start | bytes 405512 | tf_op jit(solution)/shard_map/ppermute | solution.py:544
  119.1 5.1 %collective-permute-start.1 = (f32[264,128]{1,0:T(8,128)S(1)}, f32[264,128]{1,0:T(8,128)S(1)}, u32[]{:S(2)}, u32[]{:S(2)}) collective-permute-start(f32[264,128]{1,0:T(8,128)S(1)} %get-tuple-element.24.refs_0_.one_ref), channel_id=1, source_target_pairs={{0,8},{4,12},{8,0},{12,4},{16,24},{20,28},{24,16},{28,20},{1,9},{5... | collective-permute-start | bytes 405512 | tf_op jit(solution)/shard_map/ppermute | solution.py:544
  124.9 9.3 %collective-permute-start.2 = (f32[264,128]{1,0:T(8,128)S(1)}, f32[264,128]{1,0:T(8,128)S(1)}, u32[]{:S(2)}, u32[]{:S(2)}) collective-permute-start(f32[264,128]{1,0:T(8,128)S(1)} %get-tuple-element.25.refs_0_.one_ref), channel_id=1, source_target_pairs={{0,16},{4,20},{8,24},{12,28},{16,0},{20,4},{24,8},{28,12},{1,17},{... | collective-permute-start | bytes 405512 | tf_op jit(solution)/shard_map/ppermute | solution.py:544
  134.2 2.4 %collective-permute-start.3 = (f32[136,128]{1,0:T(8,128)S(1)}, f32[136,128]{1,0:T(8,128)S(1)}, u32[]{:S(2)}, u32[]{:S(2)}) collective-permute-start(f32[136,128]{1,0:T(8,128)S(1)} %get-tuple-element.27), channel_id=1, source_target_pairs={{0,1},{1,2},{2,3},{3,0},{4,5},{5,6},{6,7},{7,4},{8,9},{9,10},{10,1... | collective-permute-start | bytes 208904 | tf_op jit(solution)/shard_map/ppermute | solution.py:532
  147.6 31.6 %collective-permute-start.6 = (f32[2048,128]{1,0:T(8,128)S(1)}, f32[2048,128]{1,0:T(8,128)S(1)}, u32[]{:S(2)}, u32[]{:S(2)}) collective-permute-start(f32[2048,128]{1,0:T(8,128)S(1)} %get-tuple-element.32.refs_0_), channel_id=1, source_target_pairs={{0,3},{1,0},{2,1},{3,2},{4,7},{5,4},{6,5},{7,6},{8,11},{9,8},{10,9... | collective-permute-start | bytes 3145736 | tf_op jit(solution)/shard_map/ppermute | solution.py:532
  149.6 5.0 %collective-permute-start.5 = (f32[264,128]{1,0:T(8,128)S(1)}, f32[264,128]{1,0:T(8,128)S(1)}, u32[]{:S(2)}, u32[]{:S(2)}) collective-permute-start(f32[264,128]{1,0:T(8,128)S(1)} %second_sums.1._.one_ref), channel_id=1, source_target_pairs={{0,4},{4,0},{8,12},{12,8},{16,20},{20,16},{24,28},{28,24},{1,5},{5... | collective-permute-start | bytes 405512 | tf_op jit(solution)/shard_map/ppermute | solution.py:544
  155.3 5.0 %collective-permute-start.7 = (f32[264,128]{1,0:T(8,128)S(1)}, f32[264,128]{1,0:T(8,128)S(1)}, u32[]{:S(2)}, u32[]{:S(2)}) collective-permute-start(f32[264,128]{1,0:T(8,128)S(1)} %get-tuple-element.33._.one_ref), channel_id=1, source_target_pairs={{0,8},{4,12},{8,0},{12,4},{16,24},{20,28},{24,16},{28,20},{1,9},{5... | collective-permute-start | bytes 405512 | tf_op jit(solution)/shard_map/ppermute | solution.py:544
  160.9 8.1 %collective-permute-start.8 = (f32[264,128]{1,0:T(8,128)S(1)}, f32[264,128]{1,0:T(8,128)S(1)}, u32[]{:S(2)}, u32[]{:S(2)}) collective-permute-start(f32[264,128]{1,0:T(8,128)S(1)} %get-tuple-element.34.one_ref), channel_id=1, source_target_pairs={{0,16},{4,20},{8,24},{12,28},{16,0},{20,4},{24,8},{28,12},{1,17},{... | collective-permute-start | bytes 405512 | tf_op jit(solution)/shard_map/ppermute | solution.py:544
  169.0 4.4 %collective-permute-start.9 = (f32[136,128]{1,0:T(8,128)S(1)}, f32[136,128]{1,0:T(8,128)S(1)}, u32[]{:S(2)}, u32[]{:S(2)}) collective-permute-start(f32[136,128]{1,0:T(8,128)S(1)} %get-tuple-element.36), channel_id=1, source_target_pairs={{0,3},{1,0},{2,1},{3,2},{4,7},{5,4},{6,5},{7,6},{8,11},{9,8},{10,9... | collective-permute-start | bytes 208904 | tf_op jit(solution)/shard_map/ppermute | solution.py:532
